TPU v7x, 32 devices: a whole 2x2x4 slice. The times are simulated.
32 devices in a mesh: section: 4 (over z), tm: 4 (over y, x), batch: 2 (over core).
Axes of the slice: x: 2, y: 2, z: 4, core: 2. Of those that a mesh axis runs over, the one named last changes fastest.
Arguments:
- acts: bfloat16 [4, 4, 8, 6, 10240], P('section', 'batch', 'tm'), may hold values from -6 to 6
- cot: bfloat16 [4, 8, 6, 10240], P('batch', 'tm'), may hold values from -6 to 6
- spatial_weight: bfloat16 [4, 9, 64, 64], P('section'), may hold values from -0.25 to 0.25
- temporal_weight: bfloat16 [4, 3, 64, 64], P('section'), may hold values from -0.4375 to 0.4375
Outputs:
- grad_in: bfloat16 [4, 4, 8, 6, 10240], P('section', 'batch', 'tm')
- grad_spatial: float32 [4, 9, 64, 64], P('section')
- grad_temporal: float32 [4, 3, 64, 64], P('section')
All inputs are finite; a program needn't handle non-finite values.
Results may differ from a plain program's by a relative error of at most 0.012.
Values may be sent and summed in bfloat16 or wider, within the bound.
A program may use at most 128 MiB of HBM per device.

v0:
```python
import jax
import jax.numpy as jnp
from jax import lax
from jax.sharding import PartitionSpec as P

TIME_DILATION = 2


def from_behind(value, axis, steps):
    count = lax.axis_size(axis)
    first, last = (max(0, -steps), min(count, count - steps))
    return lax.ppermute(value, axis, [(source, source + steps) for source in range(first, last)])


def split_pixels(a, chans):
    return a.reshape(a.shape[:-1] + (a.shape[-1] // chans, chans))


def paired_kernel(kernel):
    return jnp.kron(jnp.eye(2, dtype=kernel.dtype), kernel)


def spatial_fwd(x, ws):
    rows, width = (x.shape[1], x.shape[2])
    chans = ws.shape[-1]
    padded = jnp.pad(x, ((0, 0), (1, 1), (chans, chans)))
    total = jnp.zeros(x.shape, jnp.float32)
    for i in range(3):
        for j in range(3):
            piece = split_pixels(padded[:, i : i + rows, j * chans : j * chans + width], 2 * chans)
            total = total + jnp.einsum(
                "nrpa,ab->nrpb",
                piece,
                paired_kernel(ws[3 * i + j]),
                preferred_element_type=jnp.float32,
            ).reshape(x.shape)
    return total


def spatial_back(gz, x, ws):
    rows, width = (x.shape[1], x.shape[2])
    chans = ws.shape[-1]
    xpad = jnp.pad(x, ((0, 0), (1, 1), (chans, chans)))
    gradient_padded = jnp.pad(gz, ((0, 0), (1, 1), (chans, chans)))
    gz_pairs = split_pixels(gz, 2 * chans)
    total = jnp.zeros(x.shape, jnp.float32)
    grads = []
    for i in range(3):
        for j in range(3):
            gpiece = split_pixels(
                gradient_padded[:, 2 - i : 2 - i + rows, (2 - j) * chans : (2 - j) * chans + width],
                2 * chans,
            )
            total = total + jnp.einsum(
                "nrpb,ab->nrpa",
                gpiece,
                paired_kernel(ws[3 * i + j]),
                preferred_element_type=jnp.float32,
            ).reshape(x.shape)
            xpiece = split_pixels(xpad[:, i : i + rows, j * chans : j * chans + width], 2 * chans)
            square = jnp.einsum(
                "nrpa,nrpb->ab", xpiece, gz_pairs, preferred_element_type=jnp.float32
            )
            grads.append(square[:chans, :chans] + square[chans:, chans:])
    return (total, jnp.stack(grads))


def temporal_back(h, gradient_piece, gradient_padded, dilation_step, wt):
    count = gradient_piece.shape[0]
    chans = wt.shape[-1]
    kernel_taps = [
        gradient_padded[2 * dilation_step : 2 * dilation_step + count],
        gradient_piece,
        gradient_padded[0:count],
    ]
    h_pix = split_pixels(h, chans)
    gh = jnp.zeros(gradient_piece.shape, jnp.float32)
    tgrads = []
    for k in range(3):
        tap = split_pixels(kernel_taps[k], chans)
        gh = gh + jnp.einsum(
            "trwd,cd->trwc", tap, wt[k], preferred_element_type=jnp.float32
        ).reshape(gradient_piece.shape)
        tgrads.append(jnp.einsum("trwc,trwd->cd", h_pix, tap, preferred_element_type=jnp.float32))
    return (gh.astype(jnp.bfloat16), jnp.stack(tgrads))


def section_backward(x, gradient_piece, ws, wt):
    dilation_step = TIME_DILATION
    z = spatial_fwd(x, ws)
    sig = jax.nn.sigmoid(z)
    h = (z * sig).astype(jnp.bfloat16)
    deriv = sig * (1.0 + z * (1.0 - sig))
    tile_gradient, h_tile = (
        lax.all_to_all(gradient_piece, "tm", split_axis=2, concat_axis=0, tiled=True),
        lax.all_to_all(h, "tm", split_axis=2, concat_axis=0, tiled=True),
    )
    gradient_padded = jnp.pad(tile_gradient, ((dilation_step, dilation_step), (0, 0), (0, 0)))
    gh_tile, tgrads = temporal_back(h_tile, tile_gradient, gradient_padded, dilation_step, wt)
    gh = lax.all_to_all(gh_tile, "tm", split_axis=0, concat_axis=2, tiled=True)
    gz = (gh.astype(jnp.float32) * deriv).astype(jnp.bfloat16)
    back, sgrads = spatial_back(gz, x, ws)
    result = (gradient_piece.astype(jnp.float32) + back).astype(jnp.bfloat16)
    return (result, sgrads, tgrads)


def body(acts, cot, spatial_weight, temporal_weight):
    section_idx = lax.axis_index("section")
    number_sections = lax.axis_size("section")
    micro = acts.shape[1]
    local_acts = acts[0]
    ws = spatial_weight[0]
    wt = temporal_weight[0]
    received = jnp.zeros(cot.shape[1:], jnp.bfloat16)
    grads_in = jnp.zeros(local_acts.shape, jnp.bfloat16)
    acc_spatial = jnp.zeros(ws.shape, jnp.float32)
    acc_temporal = jnp.zeros(wt.shape, jnp.float32)
    total_turns = micro + number_sections - 1
    for turn in range(total_turns):
        which = jnp.int32(turn) - (number_sections - 1 - section_idx)
        valid = jnp.logical_and(which >= 0, which < micro)
        clipped = jnp.clip(which, 0, micro - 1)
        x_now = lax.dynamic_index_in_dim(local_acts, clipped, 0, keepdims=False)
        top_grad = lax.dynamic_index_in_dim(cot, clipped, 0, keepdims=False)
        incoming = jnp.where(section_idx == number_sections - 1, top_grad, received)
        result, sgrads, tgrads = section_backward(x_now, incoming, ws, wt)
        weight = valid.astype(jnp.float32)
        acc_spatial = acc_spatial + weight * sgrads
        acc_temporal = acc_temporal + weight * tgrads
        select = (jnp.arange(micro, dtype=jnp.int32) == which)[:, None, None, None]
        grads_in = jnp.where(select, result[None], grads_in)
        if turn + 1 < total_turns:
            received = from_behind(result, "section", -1)
    sum_spatial, sum_temporal = lax.psum((acc_spatial, acc_temporal), ("tm", "batch"))
    return (grads_in[None], sum_spatial[None], sum_temporal[None])


def solution(mesh):
    in_specs = (
        P("section", "batch", "tm", None, None),
        P("batch", "tm", None, None),
        P("section", None, None, None),
        P("section", None, None, None),
    )
    out_specs = (
        P("section", "batch", "tm", None, None),
        P("section", None, None, None),
        P("section", None, None, None),
    )
    return jax.shard_map(body, mesh=mesh, in_specs=in_specs, out_specs=out_specs, check_vma=False)
```

profile of v0, /device:TPU:24, one launch (start us, length us, event | category | flops | bytes accessed | tf_op | source)
XLA Modules:
  0.0 929.5 jit_solution(14927379624928204376)
XLA Ops:
  8.3 8.2 copy.623
  16.6 10.0 %reshape.1685 = bf16[4,2,15360]{2,1,0:T(2,128)(2,1)} reshape(bf16[10240,2,6]{2,1,0:T(2,128)(2,1)} %bitcast.1159) | data formatting | bytes 491520
  26.5 4.2 all-to-all-start
  126.4 13.6 %reshape.1686 = bf16[10240,2,6]{2,1,0:T(2,128)(2,1)} reshape(bf16[4,2,15360]{2,1,0:T(2,128)(2,1)} %all-to-all-done) | data formatting | bytes 491520
  140.0 10.6 %copy.624 = bf16[2,6,4,2560]{3,0,2,1:T(2,128)(2,1)S(1)} copy(bf16[2,6,4,2560]{1,0,3,2:T(2,128)(2,1)} %bitcast.1160) | data formatting | bytes 491520 | tf_op jit(solution)/shard_map/all_to_all | solution.py:95
  153.7 4.3 all-to-all-start.1
  159.1 4.6 all-to-all-done.1
  205.2 10.3 %copy.809 = bf16[2,6,10240]{1,0,2:T(2,128)(2,1)} copy(bf16[2,6,10240]{2,0,1:T(2,128)(2,1)} %get-tuple-element.11) | data formatting | bytes 491520 | tf_op jit(solution)/shard_map/convert_element_type | solution.py:92
  215.5 9.9 %reshape.1695 = bf16[4,2,15360]{2,1,0:T(2,128)(2,1)} reshape(bf16[10240,2,6]{2,1,0:T(2,128)(2,1)} %bitcast.1161) | data formatting | bytes 491520
  233.9 8.2 copy.651
  242.1 9.9 %reshape.1687 = bf16[4,2,15360]{2,1,0:T(2,128)(2,1)} reshape(bf16[10240,2,6]{2,1,0:T(2,128)(2,1)} %bitcast.1175) | data formatting | bytes 491520
  257.1 12.6 %reshape.1696 = bf16[10240,2,6]{2,1,0:T(2,128)(2,1)} reshape(bf16[4,2,15360]{2,1,0:T(2,128)(2,1)S(1)} %all-to-all-done.10) | data formatting | bytes 491520
  269.7 12.2 %copy.902 = bf16[2,6,4,2560]{3,2,0,1:T(4,128)(2,1)S(1)} copy(bf16[2,6,4,2560]{1,0,3,2:T(2,128)(2,1)} %bitcast.1162) | data formatting | bytes 491520 | tf_op jit(solution)/shard_map/all_to_all | solution.py:96
  283.3 12.6 %reshape.1688 = bf16[10240,2,6]{2,1,0:T(2,128)(2,1)} reshape(bf16[4,2,15360]{2,1,0:T(2,128)(2,1)S(1)} %all-to-all-done.2) | data formatting | bytes 491520
  296.0 10.2 %copy.652 = bf16[2,6,4,2560]{3,0,2,1:T(2,128)(2,1)S(1)} copy(bf16[2,6,4,2560]{1,0,3,2:T(2,128)(2,1)} %bitcast.1163) | data formatting | bytes 491520 | tf_op jit(solution)/shard_map/all_to_all | solution.py:95
  314.8 4.4 all-to-all-start.3
  366.4 10.3 %copy.812 = bf16[2,6,10240]{1,0,2:T(2,128)(2,1)} copy(bf16[2,6,10240]{2,0,1:T(2,128)(2,1)} %get-tuple-element.9) | data formatting | bytes 491520 | tf_op jit(solution)/shard_map/convert_element_type | solution.py:92
  376.7 9.9 %reshape.1697 = bf16[4,2,15360]{2,1,0:T(2,128)(2,1)} reshape(bf16[10240,2,6]{2,1,0:T(2,128)(2,1)} %bitcast.1164) | data formatting | bytes 491520
  395.5 8.1 copy.679
  403.7 9.9 %reshape.1689 = bf16[4,2,15360]{2,1,0:T(2,128)(2,1)} reshape(bf16[10240,2,6]{2,1,0:T(2,128)(2,1)} %bitcast.1176) | data formatting | bytes 491520
  418.4 12.6 %reshape.1698 = bf16[10240,2,6]{2,1,0:T(2,128)(2,1)} reshape(bf16[4,2,15360]{2,1,0:T(2,128)(2,1)S(1)} %all-to-all-done.11) | data formatting | bytes 491520
  431.1 12.2 %copy.903 = bf16[2,6,4,2560]{3,2,0,1:T(4,128)(2,1)S(1)} copy(bf16[2,6,4,2560]{1,0,3,2:T(2,128)(2,1)} %bitcast.1165) | data formatting | bytes 491520 | tf_op jit(solution)/shard_map/all_to_all | solution.py:96
  444.7 12.6 %reshape.1690 = bf16[10240,2,6]{2,1,0:T(2,128)(2,1)} reshape(bf16[4,2,15360]{2,1,0:T(2,128)(2,1)S(1)} %all-to-all-done.4) | data formatting | bytes 491520
  457.3 10.2 %copy.680 = bf16[2,6,4,2560]{3,0,2,1:T(2,128)(2,1)S(1)} copy(bf16[2,6,4,2560]{1,0,3,2:T(2,128)(2,1)} %bitcast.1166) | data formatting | bytes 491520 | tf_op jit(solution)/shard_map/all_to_all | solution.py:95
  476.2 4.4 all-to-all-start.5
  525.7 10.2 %copy.815 = bf16[2,6,10240]{1,0,2:T(2,128)(2,1)} copy(bf16[2,6,10240]{2,0,1:T(2,128)(2,1)} %get-tuple-element.7) | data formatting | bytes 491520 | tf_op jit(solution)/shard_map/convert_element_type | solution.py:92
  536.0 9.9 %reshape.1699 = bf16[4,2,15360]{2,1,0:T(2,128)(2,1)} reshape(bf16[10240,2,6]{2,1,0:T(2,128)(2,1)} %bitcast.1167) | data formatting | bytes 491520
  554.6 8.1 copy.707
  562.8 9.9 %reshape.1691 = bf16[4,2,15360]{2,1,0:T(2,128)(2,1)} reshape(bf16[10240,2,6]{2,1,0:T(2,128)(2,1)} %bitcast.1177) | data formatting | bytes 491520
  577.8 12.6 %reshape.1700 = bf16[10240,2,6]{2,1,0:T(2,128)(2,1)} reshape(bf16[4,2,15360]{2,1,0:T(2,128)(2,1)S(1)} %all-to-all-done.12) | data formatting | bytes 491520
  590.4 12.2 %copy.904 = bf16[2,6,4,2560]{3,2,0,1:T(4,128)(2,1)S(1)} copy(bf16[2,6,4,2560]{1,0,3,2:T(2,128)(2,1)} %bitcast.1168) | data formatting | bytes 491520 | tf_op jit(solution)/shard_map/all_to_all | solution.py:96
  604.0 12.6 %reshape.1692 = bf16[10240,2,6]{2,1,0:T(2,128)(2,1)} reshape(bf16[4,2,15360]{2,1,0:T(2,128)(2,1)S(1)} %all-to-all-done.6) | data formatting | bytes 491520
  616.6 10.2 %copy.708 = bf16[2,6,4,2560]{3,0,2,1:T(2,128)(2,1)S(1)} copy(bf16[2,6,4,2560]{1,0,3,2:T(2,128)(2,1)} %bitcast.1169) | data formatting | bytes 491520 | tf_op jit(solution)/shard_map/all_to_all | solution.py:95
  635.5 4.6 all-to-all-start.7
  687.6 10.2 %copy.818 = bf16[2,6,10240]{1,0,2:T(2,128)(2,1)} copy(bf16[2,6,10240]{2,0,1:T(2,128)(2,1)} %get-tuple-element.5) | data formatting | bytes 491520 | tf_op jit(solution)/shard_map/convert_element_type | solution.py:92
  697.8 9.9 %reshape.1701 = bf16[4,2,15360]{2,1,0:T(2,128)(2,1)} reshape(bf16[10240,2,6]{2,1,0:T(2,128)(2,1)} %bitcast.1170) | data formatting | bytes 491520
  712.9 8.1 copy.735
  721.1 9.9 %reshape.1693 = bf16[4,2,15360]{2,1,0:T(2,128)(2,1)} reshape(bf16[10240,2,6]{2,1,0:T(2,128)(2,1)} %bitcast.1178) | data formatting | bytes 491520
  735.9 12.6 %reshape.1702 = bf16[10240,2,6]{2,1,0:T(2,128)(2,1)} reshape(bf16[4,2,15360]{2,1,0:T(2,128)(2,1)S(1)} %all-to-all-done.13) | data formatting | bytes 491520
  748.5 12.2 %copy.905 = bf16[2,6,4,2560]{3,2,0,1:T(4,128)(2,1)S(1)} copy(bf16[2,6,4,2560]{1,0,3,2:T(2,128)(2,1)} %bitcast.1171) | data formatting | bytes 491520 | tf_op jit(solution)/shard_map/all_to_all | solution.py:96
  762.1 12.6 %reshape.1694 = bf16[10240,2,6]{2,1,0:T(2,128)(2,1)} reshape(bf16[4,2,15360]{2,1,0:T(2,128)(2,1)S(1)} %all-to-all-done.8) | data formatting | bytes 491520
  774.7 10.2 %copy.736 = bf16[2,6,4,2560]{3,0,2,1:T(2,128)(2,1)S(1)} copy(bf16[2,6,4,2560]{1,0,3,2:T(2,128)(2,1)} %bitcast.1172) | data formatting | bytes 491520 | tf_op jit(solution)/shard_map/all_to_all | solution.py:95
  788.7 4.3 all-to-all-start.9
  841.1 10.3 %copy.821 = bf16[2,6,10240]{1,0,2:T(2,128)(2,1)} copy(bf16[2,6,10240]{2,0,1:T(2,128)(2,1)} %get-tuple-element.3) | data formatting | bytes 491520 | tf_op jit(solution)/shard_map/convert_element_type | solution.py:92
  851.4 9.9 %reshape.1703 = bf16[4,2,15360]{2,1,0:T(2,128)(2,1)} reshape(bf16[10240,2,6]{2,1,0:T(2,128)(2,1)} %bitcast.1173) | data formatting | bytes 491520
  870.4 12.6 %reshape.1704 = bf16[10240,2,6]{2,1,0:T(2,128)(2,1)} reshape(bf16[4,2,15360]{2,1,0:T(2,128)(2,1)S(1)} %all-to-all-done.14) | data formatting | bytes 491520
  883.2 12.3 %copy.906 = bf16[2,6,4,2560]{3,2,0,1:T(4,128)(2,1)S(1)} copy(bf16[2,6,4,2560]{1,0,3,2:T(2,128)(2,1)} %bitcast.1174) | data formatting | bytes 491520 | tf_op jit(solution)/shard_map/all_to_all | solution.py:96
  897.0 23.7 %psum.15 = f32[1,3,64,64]{3,2,1,0:T(8,128)} all-reduce(f32[1,3,64,64]{3,2,1,0:T(8,128)S(1)} %fusion.170), channel_id=1, replica_groups=mesh['section'=4,'tm'=4,'batch'=2] {'tm','batch'}, use_global_device_ids=true, to_apply=%region_1.2 | all-reduce | flops 12288 | bytes 98304 | tf_op jit(solution)/shard_map/psum | solution.py:134
  (812 shorter events, 426.2 us)
Async XLA Ops:
  26.5 99.9 %all-to-all-start = ((bf16[4,2,15360]{2,1,0:T(2,128)(2,1)}), bf16[4,2,15360]{2,1,0:T(2,128)(2,1)}, u32[]{:S(2)}, u32[]{:S(2)}) async-start(bf16[4,2,15360]{2,1,0:T(2,128)(2,1)} %reshape.1685), calls=%async_computation | async-start | bytes 491520 | tf_op jit(solution)/shard_map/all_to_all | solution.py:95
  33.8 160.6 %copy-start.16 = (bf16[128,128,1,1]{1,0,2,3:T(8,128)(2,1)}, bf16[128,128,1,1]{1,0,2,3:T(8,128)(2,1)S(1)}, u32[]{:S(2)}) copy-start(bf16[128,128,1,1]{1,0,2,3:T(8,128)(2,1)S(1)} %reshape.1603) | copy-start | bytes 98308
  33.9 160.8 %copy-start.11 = (bf16[128,128,1,1]{1,0,2,3:T(8,128)(2,1)}, bf16[128,128,1,1]{1,0,2,3:T(8,128)(2,1)S(1)}, u32[]{:S(2)}) copy-start(bf16[128,128,1,1]{1,0,2,3:T(8,128)(2,1)S(1)} %reshape.1604) | copy-start | bytes 98308
  34.1 160.9 %copy-start.6 = (bf16[128,128,1,1]{1,0,2,3:T(8,128)(2,1)}, bf16[128,128,1,1]{1,0,2,3:T(8,128)(2,1)S(1)}, u32[]{:S(2)}) copy-start(bf16[128,128,1,1]{1,0,2,3:T(8,128)(2,1)S(1)} %reshape.1605) | copy-start | bytes 98308
  34.2 162.0 %copy-start.1 = (bf16[128,128,1,1]{1,0,2,3:T(8,128)(2,1)}, bf16[128,128,1,1]{1,0,2,3:T(8,128)(2,1)S(1)}, u32[]{:S(2)}) copy-start(bf16[128,128,1,1]{1,0,2,3:T(8,128)(2,1)S(1)} %reshape.1606) | copy-start | bytes 98308
  34.6 159.6 %copy-start.21 = (bf16[128,128,1,1]{1,0,2,3:T(8,128)(2,1)}, bf16[128,128,1,1]{1,0,2,3:T(8,128)(2,1)S(1)}, u32[]{:S(2)}) copy-start(bf16[128,128,1,1]{1,0,2,3:T(8,128)(2,1)S(1)} %reshape.1602) | copy-start | bytes 98308
  35.7 90.1 %copy-start.43 = (bf16[2,6,80,128]{3,2,0,1:T(8,128)(2,1)}, bf16[2,6,80,128]{3,2,0,1:T(8,128)(2,1)S(1)}, u32[]{:S(2)}) copy-start(bf16[2,6,80,128]{3,2,0,1:T(8,128)(2,1)S(1)} %reshape.1505) | copy-start | bytes 737284
  153.7 9.9 %all-to-all-start.1 = ((bf16[8,6,2560]{2,1,0:T(8,128)(2,1)}), bf16[8,6,2560]{2,1,0:T(8,128)(2,1)S(1)}, u32[]{:S(2)}, u32[]{:S(2)}) async-start(bf16[8,6,2560]{2,1,0:T(8,128)(2,1)} %reshape.1671), calls=%async_computation.1 | async-start | bytes 655360 | tf_op jit(solution)/shard_map/all_to_all | solution.py:100
  202.7 31.0 %collective-permute-start = (bf16[2,6,10240]{2,0,1:T(2,128)(2,1)S(1)}, bf16[2,6,10240]{2,0,1:T(2,128)(2,1)S(1)}, u32[]{:S(2)}, u32[]{:S(2)}) collective-permute-start(bf16[2,6,10240]{2,0,1:T(2,128)(2,1)S(1)} %add_convert_fusion.5), channel_id=1, source_target_pairs={{8,0},{16,8},{24,16},{9,1},{17,9},{25,17},{10,2},{18,10},{26,18},{... | collective-permute-start | bytes 737288 | tf_op jit(solution)/shard_map/ppermute | solution.py:12
  205.1 25.1 %copy-start.162 = (f32[128,128]{1,0:T(8,128)S(1)}, f32[128,128]{1,0:T(8,128)}, u32[]{:S(2)}) copy-start(f32[128,128]{1,0:T(8,128)} %convolution_bitcast_fusion.41) | copy-start | bytes 196612
  205.1 25.7 %copy-start.158 = (f32[128,128]{1,0:T(8,128)S(1)}, f32[128,128]{1,0:T(8,128)}, u32[]{:S(2)}) copy-start(f32[128,128]{1,0:T(8,128)} %convolution_bitcast_fusion.40) | copy-start | bytes 196612
  205.1 26.4 %copy-start.154 = (f32[128,128]{1,0:T(8,128)S(1)}, f32[128,128]{1,0:T(8,128)}, u32[]{:S(2)}) copy-start(f32[128,128]{1,0:T(8,128)} %convolution_bitcast_fusion.39) | copy-start | bytes 196612
  205.1 27.1 %copy-start.150 = (f32[128,128]{1,0:T(8,128)S(1)}, f32[128,128]{1,0:T(8,128)}, u32[]{:S(2)}) copy-start(f32[128,128]{1,0:T(8,128)} %convolution_bitcast_fusion.38) | copy-start | bytes 196612
  205.1 27.8 %copy-start.149 = (f32[128,128]{1,0:T(8,128)S(1)}, f32[128,128]{1,0:T(8,128)}, u32[]{:S(2)}) copy-start(f32[128,128]{1,0:T(8,128)} %convolution_bitcast_fusion.37) | copy-start | bytes 196612
  225.4 26.6 %all-to-all-start.10 = ((bf16[4,2,15360]{2,1,0:T(2,128)(2,1)}), bf16[4,2,15360]{2,1,0:T(2,128)(2,1)S(1)}, u32[]{:S(2)}, u32[]{:S(2)}) async-start(bf16[4,2,15360]{2,1,0:T(2,128)(2,1)} %reshape.1695), calls=%async_computation.10 | async-start | bytes 491520 | tf_op jit(solution)/shard_map/all_to_all | solution.py:96
  252.0 31.3 %all-to-all-start.2 = ((bf16[4,2,15360]{2,1,0:T(2,128)(2,1)}), bf16[4,2,15360]{2,1,0:T(2,128)(2,1)S(1)}, u32[]{:S(2)}, u32[]{:S(2)}) async-start(bf16[4,2,15360]{2,1,0:T(2,128)(2,1)} %reshape.1687), calls=%async_computation.2 | async-start | bytes 491520 | tf_op jit(solution)/shard_map/all_to_all | solution.py:95
  314.8 10.0 %all-to-all-start.3 = ((bf16[8,6,2560]{2,1,0:T(8,128)(2,1)}), bf16[8,6,2560]{2,1,0:T(8,128)(2,1)}, u32[]{:S(2)}, u32[]{:S(2)}) async-start(bf16[8,6,2560]{2,1,0:T(8,128)(2,1)} %reshape.1681), calls=%async_computation.3 | async-start | bytes 655360 | tf_op jit(solution)/shard_map/all_to_all | solution.py:100
  364.0 31.2 %collective-permute-start.1 = (bf16[2,6,10240]{2,0,1:T(2,128)(2,1)S(1)}, bf16[2,6,10240]{2,0,1:T(2,128)(2,1)S(1)}, u32[]{:S(2)}, u32[]{:S(2)}) collective-permute-start(bf16[2,6,10240]{2,0,1:T(2,128)(2,1)S(1)} %add_convert_fusion.4), channel_id=1, source_target_pairs={{8,0},{16,8},{24,16},{9,1},{17,9},{25,17},{10,2},{18,10},{26,18},{... | collective-permute-start | bytes 737288 | tf_op jit(solution)/shard_map/ppermute | solution.py:12
  366.4 25.4 %copy-start.167 = (f32[128,128]{1,0:T(8,128)S(1)}, f32[128,128]{1,0:T(8,128)}, u32[]{:S(2)}) copy-start(f32[128,128]{1,0:T(8,128)} %convolution_bitcast_fusion.32) | copy-start | bytes 196612
  366.4 26.1 %copy-start.163 = (f32[128,128]{1,0:T(8,128)S(1)}, f32[128,128]{1,0:T(8,128)}, u32[]{:S(2)}) copy-start(f32[128,128]{1,0:T(8,128)} %convolution_bitcast_fusion.31) | copy-start | bytes 196612
  366.4 26.8 %copy-start.159 = (f32[128,128]{1,0:T(8,128)S(1)}, f32[128,128]{1,0:T(8,128)}, u32[]{:S(2)}) copy-start(f32[128,128]{1,0:T(8,128)} %convolution_bitcast_fusion.30) | copy-start | bytes 196612
  366.4 27.4 %copy-start.155 = (f32[128,128]{1,0:T(8,128)S(1)}, f32[128,128]{1,0:T(8,128)}, u32[]{:S(2)}) copy-start(f32[128,128]{1,0:T(8,128)} %convolution_bitcast_fusion.29) | copy-start | bytes 196612
  366.4 28.1 %copy-start.151 = (f32[128,128]{1,0:T(8,128)S(1)}, f32[128,128]{1,0:T(8,128)}, u32[]{:S(2)}) copy-start(f32[128,128]{1,0:T(8,128)} %convolution_bitcast_fusion.28) | copy-start | bytes 196612
  386.6 26.9 %all-to-all-start.11 = ((bf16[4,2,15360]{2,1,0:T(2,128)(2,1)}), bf16[4,2,15360]{2,1,0:T(2,128)(2,1)S(1)}, u32[]{:S(2)}, u32[]{:S(2)}) async-start(bf16[4,2,15360]{2,1,0:T(2,128)(2,1)} %reshape.1697), calls=%async_computation.11 | async-start | bytes 491520 | tf_op jit(solution)/shard_map/all_to_all | solution.py:96
  413.6 31.1 %all-to-all-start.4 = ((bf16[4,2,15360]{2,1,0:T(2,128)(2,1)}), bf16[4,2,15360]{2,1,0:T(2,128)(2,1)S(1)}, u32[]{:S(2)}, u32[]{:S(2)}) async-start(bf16[4,2,15360]{2,1,0:T(2,128)(2,1)} %reshape.1689), calls=%async_computation.4 | async-start | bytes 491520 | tf_op jit(solution)/shard_map/all_to_all | solution.py:95
  476.2 10.0 %all-to-all-start.5 = ((bf16[8,6,2560]{2,1,0:T(8,128)(2,1)}), bf16[8,6,2560]{2,1,0:T(8,128)(2,1)}, u32[]{:S(2)}, u32[]{:S(2)}) async-start(bf16[8,6,2560]{2,1,0:T(8,128)(2,1)} %reshape.1682), calls=%async_computation.5 | async-start | bytes 655360 | tf_op jit(solution)/shard_map/all_to_all | solution.py:100
  523.5 30.9 %collective-permute-start.2 = (bf16[2,6,10240]{2,0,1:T(2,128)(2,1)S(1)}, bf16[2,6,10240]{2,0,1:T(2,128)(2,1)S(1)}, u32[]{:S(2)}, u32[]{:S(2)}) collective-permute-start(bf16[2,6,10240]{2,0,1:T(2,128)(2,1)S(1)} %add_convert_fusion.3), channel_id=1, source_target_pairs={{8,0},{16,8},{24,16},{9,1},{17,9},{25,17},{10,2},{18,10},{26,18},{... | collective-permute-start | bytes 737288 | tf_op jit(solution)/shard_map/ppermute | solution.py:12
  525.7 25.2 %copy-start.169 = (f32[128,128]{1,0:T(8,128)S(1)}, f32[128,128]{1,0:T(8,128)}, u32[]{:S(2)}) copy-start(f32[128,128]{1,0:T(8,128)} %convolution_bitcast_fusion.23) | copy-start | bytes 196612
  525.7 25.9 %copy-start.165 = (f32[128,128]{1,0:T(8,128)S(1)}, f32[128,128]{1,0:T(8,128)}, u32[]{:S(2)}) copy-start(f32[128,128]{1,0:T(8,128)} %convolution_bitcast_fusion.22) | copy-start | bytes 196612
  525.7 26.6 %copy-start.161 = (f32[128,128]{1,0:T(8,128)S(1)}, f32[128,128]{1,0:T(8,128)}, u32[]{:S(2)}) copy-start(f32[128,128]{1,0:T(8,128)} %convolution_bitcast_fusion.21) | copy-start | bytes 196612
  525.7 27.2 %copy-start.157 = (f32[128,128]{1,0:T(8,128)S(1)}, f32[128,128]{1,0:T(8,128)}, u32[]{:S(2)}) copy-start(f32[128,128]{1,0:T(8,128)} %convolution_bitcast_fusion.20) | copy-start | bytes 196612
  525.7 27.9 %copy-start.153 = (f32[128,128]{1,0:T(8,128)S(1)}, f32[128,128]{1,0:T(8,128)}, u32[]{:S(2)}) copy-start(f32[128,128]{1,0:T(8,128)} %convolution_bitcast_fusion.19) | copy-start | bytes 196612
  545.9 26.8 %all-to-all-start.12 = ((bf16[4,2,15360]{2,1,0:T(2,128)(2,1)}), bf16[4,2,15360]{2,1,0:T(2,128)(2,1)S(1)}, u32[]{:S(2)}, u32[]{:S(2)}) async-start(bf16[4,2,15360]{2,1,0:T(2,128)(2,1)} %reshape.1699), calls=%async_computation.12 | async-start | bytes 491520 | tf_op jit(solution)/shard_map/all_to_all | solution.py:96
  572.7 31.3 %all-to-all-start.6 = ((bf16[4,2,15360]{2,1,0:T(2,128)(2,1)}), bf16[4,2,15360]{2,1,0:T(2,128)(2,1)S(1)}, u32[]{:S(2)}, u32[]{:S(2)}) async-start(bf16[4,2,15360]{2,1,0:T(2,128)(2,1)} %reshape.1691), calls=%async_computation.6 | async-start | bytes 491520 | tf_op jit(solution)/shard_map/all_to_all | solution.py:95
  635.5 10.2 %all-to-all-start.7 = ((bf16[8,6,2560]{2,1,0:T(8,128)(2,1)}), bf16[8,6,2560]{2,1,0:T(8,128)(2,1)}, u32[]{:S(2)}, u32[]{:S(2)}) async-start(bf16[8,6,2560]{2,1,0:T(8,128)(2,1)} %reshape.1683), calls=%async_computation.7 | async-start | bytes 655360 | tf_op jit(solution)/shard_map/all_to_all | solution.py:100
  685.6 27.1 %collective-permute-start.3 = (bf16[2,6,10240]{2,0,1:T(2,128)(2,1)S(1)}, bf16[2,6,10240]{2,0,1:T(2,128)(2,1)S(1)}, u32[]{:S(2)}, u32[]{:S(2)}) collective-permute-start(bf16[2,6,10240]{2,0,1:T(2,128)(2,1)S(1)} %add_convert_fusion.2), channel_id=1, source_target_pairs={{8,0},{16,8},{24,16},{9,1},{17,9},{25,17},{10,2},{18,10},{26,18},{... | collective-permute-start | bytes 737288 | tf_op jit(solution)/shard_map/ppermute | solution.py:12
  687.5 24.6 %copy-start.171 = (f32[128,128]{1,0:T(8,128)S(1)}, f32[128,128]{1,0:T(8,128)}, u32[]{:S(2)}) copy-start(f32[128,128]{1,0:T(8,128)} %convolution_bitcast_fusion.15) | copy-start | bytes 196612
  687.5 24.7 %copy-start.168 = (f32[128,128]{1,0:T(8,128)S(1)}, f32[128,128]{1,0:T(8,128)}, u32[]{:S(2)}) copy-start(f32[128,128]{1,0:T(8,128)} %convolution_bitcast_fusion.14) | copy-start | bytes 196612
  687.5 24.7 %copy-start.164 = (f32[128,128]{1,0:T(8,128)S(1)}, f32[128,128]{1,0:T(8,128)}, u32[]{:S(2)}) copy-start(f32[128,128]{1,0:T(8,128)} %convolution_bitcast_fusion.13) | copy-start | bytes 196612
  687.6 24.8 %copy-start.160 = (f32[128,128]{1,0:T(8,128)S(1)}, f32[128,128]{1,0:T(8,128)}, u32[]{:S(2)}) copy-start(f32[128,128]{1,0:T(8,128)} %convolution_bitcast_fusion.12) | copy-start | bytes 196612
  687.6 24.9 %copy-start.156 = (f32[128,128]{1,0:T(8,128)S(1)}, f32[128,128]{1,0:T(8,128)}, u32[]{:S(2)}) copy-start(f32[128,128]{1,0:T(8,128)} %convolution_bitcast_fusion.11) | copy-start | bytes 196612
  687.6 25.0 %copy-start.152 = (f32[128,128]{1,0:T(8,128)S(1)}, f32[128,128]{1,0:T(8,128)}, u32[]{:S(2)}) copy-start(f32[128,128]{1,0:T(8,128)} %convolution_bitcast_fusion.10) | copy-start | bytes 196612
  707.7 23.3 %all-to-all-start.13 = ((bf16[4,2,15360]{2,1,0:T(2,128)(2,1)}), bf16[4,2,15360]{2,1,0:T(2,128)(2,1)S(1)}, u32[]{:S(2)}, u32[]{:S(2)}) async-start(bf16[4,2,15360]{2,1,0:T(2,128)(2,1)} %reshape.1701), calls=%async_computation.13 | async-start | bytes 491520 | tf_op jit(solution)/shard_map/all_to_all | solution.py:96
  731.0 31.1 %all-to-all-start.8 = ((bf16[4,2,15360]{2,1,0:T(2,128)(2,1)}), bf16[4,2,15360]{2,1,0:T(2,128)(2,1)S(1)}, u32[]{:S(2)}, u32[]{:S(2)}) async-start(bf16[4,2,15360]{2,1,0:T(2,128)(2,1)} %reshape.1693), calls=%async_computation.8 | async-start | bytes 491520 | tf_op jit(solution)/shard_map/all_to_all | solution.py:95
  735.9 24.8 %copy-start.122 = (f32[9,64,64]{2,1,0:T(8,128)}, f32[9,64,64]{2,1,0:T(8,128)S(1)}, u32[]{:S(2)}) copy-start(f32[9,64,64]{2,1,0:T(8,128)S(1)} %get-tuple-element.143) | copy-start | bytes 442372
  788.7 9.9 %all-to-all-start.9 = ((bf16[8,6,2560]{2,1,0:T(8,128)(2,1)}), bf16[8,6,2560]{2,1,0:T(8,128)(2,1)S(1)}, u32[]{:S(2)}, u32[]{:S(2)}) async-start(bf16[8,6,2560]{2,1,0:T(8,128)(2,1)} %reshape.1684), calls=%async_computation.9 | async-start | bytes 655360 | tf_op jit(solution)/shard_map/all_to_all | solution.py:100
  793.0 127.7 %all-reduce.17.cloned.1.call-start = ((), (), s32[]{:S(2)}) async-start(), calls=%async_computation.15 | async-start | bytes 589824 | tf_op jit(solution)/shard_map/psum | solution.py:134
  861.3 9.1 all-to-all-start.14
  (151 other events, 1933.2 us)
Sparse Core Ops, SparseCore 0:
  820.6 53.1 all-reduce.16
where the time goes:
time: 944 us; the launch traced here: 930 us
  local copies, waits for them, and re-layouts  609 us (65%)
  matrix products  137 us (15%)
  starting transfers between devices  70 us (7%)
  other arithmetic  49 us (5%)
  blocking collectives  23.7 us (3%)
  waiting for transfers between devices  23.2 us (2%)
  between operations  17.9 us (2%)
    unnamed x379, local copies, waits for them, and re-layouts  229 us
    reshape x105, local copies, waits for them, and re-layouts, split_pixels(): return a.reshape(a.shape[:-1] + (a.shape[-1] // chans, chans))  112 us
    all_to_all x10, local copies, waits for them, and re-layouts, section_backward(): lax.all_to_all(h, 'tm', split_axis=2, concat_axis=0, tiled=True)  61.8 us
    dot_general x45, matrix products, spatial_back(): jnp.einsum('nrpa,nrpb->ab', xpiece, gz_pairs, preferred_element_type=jnp....  54.5 us
    all_to_all x10, local copies, waits for them, and re-layouts, section_backward(): lax.all_to_all(gradient_piece, 'tm', split_axis=2, concat_axis=0, tiled=T...  52.1 us
    convert_element_type x5, local copies, waits for them, and re-layouts, section_backward(): h = (z * sig).astype(jnp.bfloat16)  51.3 us
    select_n x5, local copies, waits for them, and re-layouts, body(): incoming = jnp.where(section_idx == number_sections - 1, top_grad, received)  40.8 us
    dot_general x45, matrix products, spatial_fwd(): jnp.einsum('nrpa,ab->nrpb', piece, paired_kernel(ws[3 * i + j]), preferre...  28.6 us
  transfers between devices with their start and end apart: 20, of which 6 were waited for; matrix products, arithmetic and copies ran while one was open for 48% of the time, Pallas kernels for 0%

commit v1 on v0

--- a/solution.py
+++ b/solution.py
@@ -4,6 +4,22 @@
 from jax.sharding import PartitionSpec as P
 
 TIME_DILATION = 2
+
+
+def pairwise_exchange(x, axis, split, join):
+    ways, here = (lax.axis_size(axis), lax.axis_index(axis))
+    width = x.shape[split] // ways
+    lengths = list(x.shape)
+    lengths[split] = width
+    height = lengths[join]
+    lengths[join] = height * ways
+    full = jnp.zeros(lengths, x.dtype)
+    for mask in range(ways):
+        part = lax.dynamic_slice_in_dim(x, (here ^ mask) * width, width, axis=split)
+        if mask:
+            part = lax.ppermute(part, axis, [(d, d ^ mask) for d in range(ways)])
+        full = lax.dynamic_update_slice_in_dim(full, part, (here ^ mask) * height, axis=join)
+    return full
 
 
 def from_behind(value, axis, steps):
@@ -92,7 +108,7 @@
     h = (z * sig).astype(jnp.bfloat16)
     deriv = sig * (1.0 + z * (1.0 - sig))
     tile_gradient, h_tile = (
-        lax.all_to_all(gradient_piece, "tm", split_axis=2, concat_axis=0, tiled=True),
+        pairwise_exchange(gradient_piece, "tm", 2, 0),
         lax.all_to_all(h, "tm", split_axis=2, concat_axis=0, tiled=True),
     )
     gradient_padded = jnp.pad(tile_gradient, ((dilation_step, dilation_step), (0, 0), (0, 0)))

time: 944 us -> 769 us (0.81)
  local copies, waits for them, and re-layouts: 609 us -> 413 us
  waiting for transfers between devices: 23.2 us -> 42.1 us
    unnamed x379 -> x339, local copies, waits for them, and re-layouts: 229 us -> 116 us
    all_to_all x10 -> x0, local copies, waits for them, and re-layouts: 52.1 us -> none  [section_backward(): lax.all_to_all(gradient_piece, 'tm', split_axis=2, concat_axis=0, tiled=T...]
    select_n x5 -> x0, local copies, waits for them, and re-layouts: 40.8 us -> none  [body(): incoming = jnp.where(section_idx == number_sections - 1, top_grad, received)]
    all_to_all x5 -> x0, starting transfers between devices: 20.8 us -> none  [section_backward(): lax.all_to_all(gradient_piece, 'tm', split_axis=2, concat_axis=0, tiled=T...]
    ppermute x0 -> x15, starting transfers between devices: none -> 17.7 us  [pairwise_exchange(): part = lax.ppermute(part, axis, [(d, d ^ mask) for d in range(ways)])]
    ppermute x0 -> x15, waiting for transfers between devices: none -> 14.7 us  [pairwise_exchange(): part = lax.ppermute(part, axis, [(d, d ^ mask) for d in range(ways)])]
  transfers between devices with their start and end apart: 20 -> 30, of which waited for: 6 -> 14; matrix products, arithmetic and copies ran while one was open for 48% -> 50% of each run, Pallas kernels for 0% -> 0%
where the time goes in v1:
time: 769 us; the launch traced here: 754 us
  local copies, waits for them, and re-layouts  413 us (54%)
  matrix products  146 us (19%)
  starting transfers between devices  64.8 us (8%)
  other arithmetic  46.4 us (6%)
  waiting for transfers between devices  42.1 us (5%)
  blocking collectives  23.7 us (3%)
  between operations  17.9 us (2%)
    unnamed x339, local copies, waits for them, and re-layouts  116 us
    reshape x105, local copies, waits for them, and re-layouts, split_pixels(): return a.reshape(a.shape[:-1] + (a.shape[-1] // chans, chans))  113 us
    all_to_all x10, local copies, waits for them, and re-layouts, section_backward(): lax.all_to_all(h, 'tm', split_axis=2, concat_axis=0, tiled=True)  61.8 us
    dot_general x45, matrix products, spatial_back(): jnp.einsum('nrpa,nrpb->ab', xpiece, gz_pairs, preferred_element_type=jnp....  60.6 us
    convert_element_type x5, local copies, waits for them, and re-layouts, section_backward(): h = (z * sig).astype(jnp.bfloat16)  51.2 us
    dot_general x45, matrix products, spatial_fwd(): jnp.einsum('nrpa,ab->nrpb', piece, paired_kernel(ws[3 * i + j]), preferre...  30.1 us
    dot_general x45, matrix products, spatial_back(): jnp.einsum('nrpb,ab->nrpa', gpiece, paired_kernel(ws[3 * i + j]), preferr...  28.4 us
    unnamed x40, other arithmetic  24.2 us
  transfers between devices with their start and end apart: 30, of which 14 were waited for; matrix products, arithmetic and copies ran while one was open for 50% of the time, Pallas kernels for 0%

profile of v1, /device:TPU:24, one launch (start us, length us, event | category | flops | bytes accessed | tf_op | source)
XLA Modules:
  0.0 754.0 jit_solution(12272145761379048959)
XLA Ops:
  22.3 3.2 pad_slice_fusion.34
  45.0 3.0 pad_slice_fusion.66
  59.0 3.0 pad_slice_fusion.50
  74.1 3.6 pad_slice_fusion.18
  117.3 3.9 all-to-all-start
  122.3 4.5 all-to-all-done
  172.9 10.3 %copy.790 = bf16[2,6,10240]{1,0,2:T(2,128)(2,1)} copy(bf16[2,6,10240]{2,0,1:T(2,128)(2,1)} %get-tuple-element.11) | data formatting | bytes 491520 | tf_op jit(solution)/shard_map/convert_element_type | solution.py:108
  183.2 9.9 %reshape.1687 = bf16[4,2,15360]{2,1,0:T(2,128)(2,1)} reshape(bf16[10240,2,6]{2,1,0:T(2,128)(2,1)} %bitcast.1139) | data formatting | bytes 491520
  193.1 3.8 all-to-all-start.5
  202.2 12.7 %reshape.1688 = bf16[10240,2,6]{2,1,0:T(2,128)(2,1)} reshape(bf16[4,2,15360]{2,1,0:T(2,128)(2,1)S(1)} %all-to-all-done.5) | data formatting | bytes 491520
  214.9 12.2 %copy.883 = bf16[2,6,4,2560]{3,2,0,1:T(4,128)(2,1)S(1)} copy(bf16[2,6,4,2560]{1,0,3,2:T(2,128)(2,1)} %bitcast.1140) | data formatting | bytes 491520 | tf_op jit(solution)/shard_map/all_to_all | solution.py:112
  232.7 3.7 collective-permute-done.5
  246.2 4.1 all-to-all-start.1
  252.1 3.8 all-to-all-done.1
  275.9 3.0 pad_slice_fusion.58
  298.2 10.2 %copy.793 = bf16[2,6,10240]{1,0,2:T(2,128)(2,1)} copy(bf16[2,6,10240]{2,0,1:T(2,128)(2,1)} %get-tuple-element.9) | data formatting | bytes 491520 | tf_op jit(solution)/shard_map/convert_element_type | solution.py:108
  308.4 9.9 %reshape.1689 = bf16[4,2,15360]{2,1,0:T(2,128)(2,1)} reshape(bf16[10240,2,6]{2,1,0:T(2,128)(2,1)} %bitcast.1141) | data formatting | bytes 491520
  318.3 3.6 all-to-all-start.6
  327.2 12.7 %reshape.1690 = bf16[10240,2,6]{2,1,0:T(2,128)(2,1)} reshape(bf16[4,2,15360]{2,1,0:T(2,128)(2,1)S(1)} %all-to-all-done.6) | data formatting | bytes 491520
  339.9 12.2 %copy.884 = bf16[2,6,4,2560]{3,2,0,1:T(4,128)(2,1)S(1)} copy(bf16[2,6,4,2560]{1,0,3,2:T(2,128)(2,1)} %bitcast.1142) | data formatting | bytes 491520 | tf_op jit(solution)/shard_map/all_to_all | solution.py:112
  357.7 3.4 collective-permute-done.9
  369.8 4.1 all-to-all-start.2
  375.7 3.8 all-to-all-done.2
  421.8 10.3 %copy.796 = bf16[2,6,10240]{1,0,2:T(2,128)(2,1)} copy(bf16[2,6,10240]{2,0,1:T(2,128)(2,1)} %get-tuple-element.7) | data formatting | bytes 491520 | tf_op jit(solution)/shard_map/convert_element_type | solution.py:108
  432.1 9.9 %reshape.1691 = bf16[4,2,15360]{2,1,0:T(2,128)(2,1)} reshape(bf16[10240,2,6]{2,1,0:T(2,128)(2,1)} %bitcast.1143) | data formatting | bytes 491520
  442.0 3.8 all-to-all-start.7
  451.1 12.7 %reshape.1692 = bf16[10240,2,6]{2,1,0:T(2,128)(2,1)} reshape(bf16[4,2,15360]{2,1,0:T(2,128)(2,1)S(1)} %all-to-all-done.7) | data formatting | bytes 491520
  463.8 12.2 %copy.885 = bf16[2,6,4,2560]{3,2,0,1:T(4,128)(2,1)S(1)} copy(bf16[2,6,4,2560]{1,0,3,2:T(2,128)(2,1)} %bitcast.1144) | data formatting | bytes 491520 | tf_op jit(solution)/shard_map/all_to_all | solution.py:112
  481.6 3.8 collective-permute-done.13
  494.1 4.1 all-to-all-start.3
  500.0 3.8 all-to-all-done.3
  523.8 3.0 pad_slice_fusion.26
  545.6 10.2 %copy.799 = bf16[2,6,10240]{1,0,2:T(2,128)(2,1)} copy(bf16[2,6,10240]{2,0,1:T(2,128)(2,1)} %get-tuple-element.5) | data formatting | bytes 491520 | tf_op jit(solution)/shard_map/convert_element_type | solution.py:108
  555.8 9.9 %reshape.1693 = bf16[4,2,15360]{2,1,0:T(2,128)(2,1)} reshape(bf16[10240,2,6]{2,1,0:T(2,128)(2,1)} %bitcast.1145) | data formatting | bytes 491520
  565.7 3.6 all-to-all-start.8
  574.6 12.7 %reshape.1694 = bf16[10240,2,6]{2,1,0:T(2,128)(2,1)} reshape(bf16[4,2,15360]{2,1,0:T(2,128)(2,1)S(1)} %all-to-all-done.8) | data formatting | bytes 491520
  587.3 12.2 %copy.886 = bf16[2,6,4,2560]{3,2,0,1:T(4,128)(2,1)S(1)} copy(bf16[2,6,4,2560]{1,0,3,2:T(2,128)(2,1)} %bitcast.1146) | data formatting | bytes 491520 | tf_op jit(solution)/shard_map/all_to_all | solution.py:112
  605.1 3.7 collective-permute-done.17
  614.0 3.6 all-to-all-start.4
  619.5 3.6 all-to-all-done.4
  646.7 3.2 pad_slice_fusion.10
  665.8 10.2 %copy.802 = bf16[2,6,10240]{1,0,2:T(2,128)(2,1)} copy(bf16[2,6,10240]{2,0,1:T(2,128)(2,1)} %get-tuple-element.3) | data formatting | bytes 491520 | tf_op jit(solution)/shard_map/convert_element_type | solution.py:108
  676.1 9.9 %reshape.1695 = bf16[4,2,15360]{2,1,0:T(2,128)(2,1)} reshape(bf16[10240,2,6]{2,1,0:T(2,128)(2,1)} %bitcast.1147) | data formatting | bytes 491520
  686.0 3.4 all-to-all-start.9
  691.2 3.6 all-to-all-done.9
  694.8 12.7 %reshape.1696 = bf16[10240,2,6]{2,1,0:T(2,128)(2,1)} reshape(bf16[4,2,15360]{2,1,0:T(2,128)(2,1)S(1)} %all-to-all-done.9) | data formatting | bytes 491520
  707.6 12.3 %copy.887 = bf16[2,6,4,2560]{3,2,0,1:T(4,128)(2,1)S(1)} copy(bf16[2,6,4,2560]{1,0,3,2:T(2,128)(2,1)} %bitcast.1148) | data formatting | bytes 491520 | tf_op jit(solution)/shard_map/all_to_all | solution.py:112
  721.5 23.7 %psum.15 = f32[1,3,64,64]{3,2,1,0:T(8,128)} all-reduce(f32[1,3,64,64]{3,2,1,0:T(8,128)S(1)} %fusion.173), channel_id=1, replica_groups=mesh['section'=4,'tm'=4,'batch'=2] {'tm','batch'}, use_global_device_ids=true, to_apply=%region_1.2 | all-reduce | flops 12288 | bytes 98304 | tf_op jit(solution)/shard_map/psum | solution.py:150
  (803 shorter events, 389.6 us)
Async XLA Ops:
  9.8 104.5 %collective-permute-start.2 = (bf16[2,6,2560]{2,0,1:T(2,128)(2,1)S(1)}, bf16[2,6,2560]{2,0,1:T(2,128)(2,1)S(1)}, u32[]{:S(2)}, u32[]{:S(2)}) collective-permute-start(bf16[2,6,2560]{2,0,1:T(2,128)(2,1)S(1)} %get-tuple-element.124), channel_id=1, source_target_pairs={{0,6},{2,4},{4,2},{6,0},{1,7},{3,5},{5,3},{7,1},{8,14},{10,12},{12... | collective-permute-start | bytes 184328 | tf_op jit(solution)/shard_map/ppermute | solution.py:20
  12.3 101.1 %collective-permute-start.1 = (bf16[2,6,2560]{2,0,1:T(2,128)(2,1)}, bf16[2,6,2560]{2,0,1:T(2,128)(2,1)}, u32[]{:S(2)}, u32[]{:S(2)}) collective-permute-start(bf16[2,6,2560]{2,0,1:T(2,128)(2,1)} %get-tuple-element.125), channel_id=1, source_target_pairs={{0,4},{2,6},{4,0},{6,2},{1,5},{3,7},{5,1},{7,3},{8,12},{10,14},{12... | collective-permute-start | bytes 184328 | tf_op jit(solution)/shard_map/ppermute | solution.py:20
  12.8 99.7 %collective-permute-start = (bf16[2,6,2560]{2,0,1:T(2,128)(2,1)}, bf16[2,6,2560]{2,0,1:T(2,128)(2,1)}, u32[]{:S(2)}, u32[]{:S(2)}) collective-permute-start(bf16[2,6,2560]{2,0,1:T(2,128)(2,1)} %get-tuple-element.126), channel_id=1, source_target_pairs={{0,2},{2,0},{4,6},{6,4},{1,3},{3,1},{5,7},{7,5},{8,10},{10,8},{12,... | collective-permute-start | bytes 184328 | tf_op jit(solution)/shard_map/ppermute | solution.py:20
  15.6 146.6 %copy-start.16 = (bf16[128,128,1,1]{1,0,2,3:T(8,128)(2,1)}, bf16[128,128,1,1]{1,0,2,3:T(8,128)(2,1)S(1)}, u32[]{:S(2)}) copy-start(bf16[128,128,1,1]{1,0,2,3:T(8,128)(2,1)S(1)} %reshape.1605) | copy-start | bytes 98308
  15.7 146.8 %copy-start.11 = (bf16[128,128,1,1]{1,0,2,3:T(8,128)(2,1)}, bf16[128,128,1,1]{1,0,2,3:T(8,128)(2,1)S(1)}, u32[]{:S(2)}) copy-start(bf16[128,128,1,1]{1,0,2,3:T(8,128)(2,1)S(1)} %reshape.1606) | copy-start | bytes 98308
  15.8 146.9 %copy-start.6 = (bf16[128,128,1,1]{1,0,2,3:T(8,128)(2,1)}, bf16[128,128,1,1]{1,0,2,3:T(8,128)(2,1)S(1)}, u32[]{:S(2)}) copy-start(bf16[128,128,1,1]{1,0,2,3:T(8,128)(2,1)S(1)} %reshape.1607) | copy-start | bytes 98308
  15.9 148.0 %copy-start.1 = (bf16[128,128,1,1]{1,0,2,3:T(8,128)(2,1)}, bf16[128,128,1,1]{1,0,2,3:T(8,128)(2,1)S(1)}, u32[]{:S(2)}) copy-start(bf16[128,128,1,1]{1,0,2,3:T(8,128)(2,1)S(1)} %reshape.1608) | copy-start | bytes 98308
  16.3 145.6 %copy-start.21 = (bf16[128,128,1,1]{1,0,2,3:T(8,128)(2,1)}, bf16[128,128,1,1]{1,0,2,3:T(8,128)(2,1)S(1)}, u32[]{:S(2)}) copy-start(bf16[128,128,1,1]{1,0,2,3:T(8,128)(2,1)S(1)} %reshape.1604) | copy-start | bytes 98308
  18.9 91.4 %copy-start.41 = (bf16[2,6,80,128]{3,2,0,1:T(8,128)(2,1)}, bf16[2,6,80,128]{3,2,0,1:T(8,128)(2,1)S(1)}, u32[]{:S(2)}) copy-start(bf16[2,6,80,128]{3,2,0,1:T(8,128)(2,1)S(1)} %reshape.1506) | copy-start | bytes 737284
  117.3 9.4 %all-to-all-start = ((bf16[8,6,2560]{2,1,0:T(8,128)(2,1)}), bf16[8,6,2560]{2,1,0:T(8,128)(2,1)S(1)}, u32[]{:S(2)}, u32[]{:S(2)}) async-start(bf16[8,6,2560]{2,1,0:T(8,128)(2,1)} %reshape.1673), calls=%async_computation | async-start | bytes 655360 | tf_op jit(solution)/shard_map/all_to_all | solution.py:116
  170.4 57.1 %collective-permute-start.3 = (bf16[2,6,10240]{2,0,1:T(2,128)(2,1)S(1)}, bf16[2,6,10240]{2,0,1:T(2,128)(2,1)S(1)}, u32[]{:S(2)}, u32[]{:S(2)}) collective-permute-start(bf16[2,6,10240]{2,0,1:T(2,128)(2,1)S(1)} %fusion.6), channel_id=1, source_target_pairs={{8,0},{16,8},{24,16},{9,1},{17,9},{25,17},{10,2},{18,10},{26,18},{... | collective-permute-start | bytes 737288 | tf_op jit(solution)/shard_map/ppermute | solution.py:28
  172.9 26.8 %copy-start.146 = (f32[128,128]{1,0:T(8,128)S(1)}, f32[128,128]{1,0:T(8,128)}, u32[]{:S(2)}) copy-start(f32[128,128]{1,0:T(8,128)} %convolution_bitcast_fusion.39) | copy-start | bytes 196612
  172.9 27.5 %copy-start.142 = (f32[128,128]{1,0:T(8,128)S(1)}, f32[128,128]{1,0:T(8,128)}, u32[]{:S(2)}) copy-start(f32[128,128]{1,0:T(8,128)} %convolution_bitcast_fusion.38) | copy-start | bytes 196612
  172.9 28.1 %copy-start.141 = (f32[128,128]{1,0:T(8,128)S(1)}, f32[128,128]{1,0:T(8,128)}, u32[]{:S(2)}) copy-start(f32[128,128]{1,0:T(8,128)} %convolution_bitcast_fusion.37) | copy-start | bytes 196612
  193.1 9.1 %all-to-all-start.5 = ((bf16[4,2,15360]{2,1,0:T(2,128)(2,1)}), bf16[4,2,15360]{2,1,0:T(2,128)(2,1)S(1)}, u32[]{:S(2)}, u32[]{:S(2)}) async-start(bf16[4,2,15360]{2,1,0:T(2,128)(2,1)} %reshape.1687), calls=%async_computation.5 | async-start | bytes 491520 | tf_op jit(solution)/shard_map/all_to_all | solution.py:112
  228.1 4.5 collective-permute-start.4
  230.6 5.9 collective-permute-start.6
  232.1 4.3 collective-permute-start.5
  246.2 9.7 %all-to-all-start.1 = ((bf16[8,6,2560]{2,1,0:T(8,128)(2,1)}), bf16[8,6,2560]{2,1,0:T(8,128)(2,1)}, u32[]{:S(2)}, u32[]{:S(2)}) async-start(bf16[8,6,2560]{2,1,0:T(8,128)(2,1)} %reshape.1683), calls=%async_computation.1 | async-start | bytes 655360 | tf_op jit(solution)/shard_map/all_to_all | solution.py:116
  295.8 56.8 %collective-permute-start.7 = (bf16[2,6,10240]{2,0,1:T(2,128)(2,1)S(1)}, bf16[2,6,10240]{2,0,1:T(2,128)(2,1)S(1)}, u32[]{:S(2)}, u32[]{:S(2)}) collective-permute-start(bf16[2,6,10240]{2,0,1:T(2,128)(2,1)S(1)} %add_convert_fusion.3), channel_id=1, source_target_pairs={{8,0},{16,8},{24,16},{9,1},{17,9},{25,17},{10,2},{18,10},{26,18},{... | collective-permute-start | bytes 737288 | tf_op jit(solution)/shard_map/ppermute | solution.py:28
  298.2 26.5 %copy-start.143 = (f32[128,128]{1,0:T(8,128)S(1)}, f32[128,128]{1,0:T(8,128)}, u32[]{:S(2)}) copy-start(f32[128,128]{1,0:T(8,128)} %convolution_bitcast_fusion.28) | copy-start | bytes 196612
  298.2 26.6 %copy-start.137 = (f32[128,128]{1,0:T(8,128)S(1)}, f32[128,128]{1,0:T(8,128)}, u32[]{:S(2)}) copy-start(f32[128,128]{1,0:T(8,128)} %convolution_bitcast_fusion.36) | copy-start | bytes 196612
  298.2 26.6 %copy-start.139 = (f32[128,128]{1,0:T(8,128)S(1)}, f32[128,128]{1,0:T(8,128)}, u32[]{:S(2)}) copy-start(f32[128,128]{1,0:T(8,128)} %convolution_bitcast_fusion.27) | copy-start | bytes 196612
  318.3 8.9 %all-to-all-start.6 = ((bf16[4,2,15360]{2,1,0:T(2,128)(2,1)}), bf16[4,2,15360]{2,1,0:T(2,128)(2,1)S(1)}, u32[]{:S(2)}, u32[]{:S(2)}) async-start(bf16[4,2,15360]{2,1,0:T(2,128)(2,1)} %reshape.1689), calls=%async_computation.6 | async-start | bytes 491520 | tf_op jit(solution)/shard_map/all_to_all | solution.py:112
  353.1 4.5 collective-permute-start.8
  355.3 5.9 collective-permute-start.10
  356.8 4.3 collective-permute-start.9
  369.8 9.7 %all-to-all-start.2 = ((bf16[8,6,2560]{2,1,0:T(8,128)(2,1)}), bf16[8,6,2560]{2,1,0:T(8,128)(2,1)}, u32[]{:S(2)}, u32[]{:S(2)}) async-start(bf16[8,6,2560]{2,1,0:T(8,128)(2,1)} %reshape.1684), calls=%async_computation.2 | async-start | bytes 655360 | tf_op jit(solution)/shard_map/all_to_all | solution.py:116
  419.4 57.1 %collective-permute-start.11 = (bf16[2,6,10240]{2,0,1:T(2,128)(2,1)S(1)}, bf16[2,6,10240]{2,0,1:T(2,128)(2,1)S(1)}, u32[]{:S(2)}, u32[]{:S(2)}) collective-permute-start(bf16[2,6,10240]{2,0,1:T(2,128)(2,1)S(1)} %add_convert_fusion.2), channel_id=1, source_target_pairs={{8,0},{16,8},{24,16},{9,1},{17,9},{25,17},{10,2},{18,10},{26,18},{... | collective-permute-start | bytes 737288 | tf_op jit(solution)/shard_map/ppermute | solution.py:28
  421.8 26.8 %copy-start.152 = (f32[128,128]{1,0:T(8,128)S(1)}, f32[128,128]{1,0:T(8,128)}, u32[]{:S(2)}) copy-start(f32[128,128]{1,0:T(8,128)} %convolution_bitcast_fusion.21) | copy-start | bytes 196612
  421.8 27.5 %copy-start.148 = (f32[128,128]{1,0:T(8,128)S(1)}, f32[128,128]{1,0:T(8,128)}, u32[]{:S(2)}) copy-start(f32[128,128]{1,0:T(8,128)} %convolution_bitcast_fusion.20) | copy-start | bytes 196612
  421.8 28.2 %copy-start.144 = (f32[128,128]{1,0:T(8,128)S(1)}, f32[128,128]{1,0:T(8,128)}, u32[]{:S(2)}) copy-start(f32[128,128]{1,0:T(8,128)} %convolution_bitcast_fusion.19) | copy-start | bytes 196612
  442.0 9.1 %all-to-all-start.7 = ((bf16[4,2,15360]{2,1,0:T(2,128)(2,1)}), bf16[4,2,15360]{2,1,0:T(2,128)(2,1)S(1)}, u32[]{:S(2)}, u32[]{:S(2)}) async-start(bf16[4,2,15360]{2,1,0:T(2,128)(2,1)} %reshape.1691), calls=%async_computation.7 | async-start | bytes 491520 | tf_op jit(solution)/shard_map/all_to_all | solution.py:112
  477.0 4.5 collective-permute-start.12
  479.6 5.9 collective-permute-start.14
  481.1 4.3 collective-permute-start.13
  494.1 9.7 %all-to-all-start.3 = ((bf16[8,6,2560]{2,1,0:T(8,128)(2,1)}), bf16[8,6,2560]{2,1,0:T(8,128)(2,1)}, u32[]{:S(2)}, u32[]{:S(2)}) async-start(bf16[8,6,2560]{2,1,0:T(8,128)(2,1)} %reshape.1685), calls=%async_computation.3 | async-start | bytes 655360 | tf_op jit(solution)/shard_map/all_to_all | solution.py:116
  543.6 56.3 %collective-permute-start.15 = (bf16[2,6,10240]{2,0,1:T(2,128)(2,1)S(1)}, bf16[2,6,10240]{2,0,1:T(2,128)(2,1)S(1)}, u32[]{:S(2)}, u32[]{:S(2)}) collective-permute-start(bf16[2,6,10240]{2,0,1:T(2,128)(2,1)S(1)} %add_convert_fusion.1), channel_id=1, source_target_pairs={{8,0},{16,8},{24,16},{9,1},{17,9},{25,17},{10,2},{18,10},{26,18},{... | collective-permute-start | bytes 737288 | tf_op jit(solution)/shard_map/ppermute | solution.py:28
  545.6 26.5 %copy-start.145 = (f32[128,128]{1,0:T(8,128)S(1)}, f32[128,128]{1,0:T(8,128)}, u32[]{:S(2)}) copy-start(f32[128,128]{1,0:T(8,128)} %convolution_bitcast_fusion.10) | copy-start | bytes 196612
  545.6 26.6 %copy-start.138 = (f32[128,128]{1,0:T(8,128)S(1)}, f32[128,128]{1,0:T(8,128)}, u32[]{:S(2)}) copy-start(f32[128,128]{1,0:T(8,128)} %convolution_bitcast_fusion.18) | copy-start | bytes 196612
  545.6 26.6 %copy-start.140 = (f32[128,128]{1,0:T(8,128)S(1)}, f32[128,128]{1,0:T(8,128)}, u32[]{:S(2)}) copy-start(f32[128,128]{1,0:T(8,128)} %convolution_bitcast_fusion.9) | copy-start | bytes 196612
  565.7 8.9 %all-to-all-start.8 = ((bf16[4,2,15360]{2,1,0:T(2,128)(2,1)}), bf16[4,2,15360]{2,1,0:T(2,128)(2,1)S(1)}, u32[]{:S(2)}, u32[]{:S(2)}) async-start(bf16[4,2,15360]{2,1,0:T(2,128)(2,1)} %reshape.1693), calls=%async_computation.8 | async-start | bytes 491520 | tf_op jit(solution)/shard_map/all_to_all | solution.py:112
  600.5 4.5 collective-permute-start.16
  602.7 6.2 collective-permute-start.18
  604.2 4.6 collective-permute-start.17
  614.0 9.1 %all-to-all-start.4 = ((bf16[8,6,2560]{2,1,0:T(8,128)(2,1)}), bf16[8,6,2560]{2,1,0:T(8,128)(2,1)S(1)}, u32[]{:S(2)}, u32[]{:S(2)}) async-start(bf16[8,6,2560]{2,1,0:T(8,128)(2,1)} %reshape.1686), calls=%async_computation.4 | async-start | bytes 655360 | tf_op jit(solution)/shard_map/all_to_all | solution.py:116
  617.6 127.6 %all-reduce.17.cloned.1.call-start = ((), (), s32[]{:S(2)}) async-start(), calls=%async_computation.10 | async-start | bytes 589824 | tf_op jit(solution)/shard_map/psum | solution.py:150
  686.0 8.9 %all-to-all-start.9 = ((bf16[4,2,15360]{2,1,0:T(2,128)(2,1)}), bf16[4,2,15360]{2,1,0:T(2,128)(2,1)S(1)}, u32[]{:S(2)}, u32[]{:S(2)}) async-start(bf16[4,2,15360]{2,1,0:T(2,128)(2,1)} %reshape.1695), calls=%async_computation.9 | async-start | bytes 491520 | tf_op jit(solution)/shard_map/all_to_all | solution.py:112
  (146 other events, 1851.5 us)
Sparse Core Ops, SparseCore 0:
  645.2 53.1 all-reduce.16
